TPU v7x, 32 devices: a whole 2x2x4 slice. The times are simulated.
32 devices in a mesh: groups: 2 (over x), tok: 16 (over z, y, core).
Axes of the slice: x: 2, y: 2, z: 4, core: 2. Of those that a mesh axis runs over, the one named last changes fastest.
Arguments:
- queries: bfloat16 [4096, 4096], P(('groups', 'tok')), parts along dimension 0, may hold values from -8 to 8
- new_keys: bfloat16 [4096, 512], P(('groups', 'tok')), parts along dimension 0, may hold values from -8 to 8
- new_values: bfloat16 [4096, 512], P(('groups', 'tok')), parts along dimension 0, may hold values from -6 to 6
- cache_keys: bfloat16 [65536, 512], P(('groups', 'tok')), parts along dimension 0, may hold values from -8 to 8
- cache_values: bfloat16 [65536, 512], P(('groups', 'tok')), parts along dimension 0, may hold values from -6 to 6
- cache_lens: int32 [32], P(('groups', 'tok')), parts along dimension 0, may hold values from 1 to 2048, 20480 in all
- residual: bfloat16 [4096, 2048], P(('groups', 'tok')), parts along dimension 0, may hold values from -40 to 40
- out_weight: bfloat16 [4096, 2048], P('tok'), may hold values from -0.09375 to 0.09375
- norm_gain: float32 [2048], replicated, may hold values from 0.25 to 1.75
- expert_ids: int32 [4096, 8], P(('groups', 'tok')), parts along dimension 0, may hold values from 0 to 63, all different within a row; in each aligned block of 64 rows (0 to 63, 64 to 127, ...) at most 12 rows name the same one
- route_weights: float32 [4096, 8], P(('groups', 'tok')), parts along dimension 0, may hold values from 0.2 to 1
- gate_weight: bfloat16 [64, 2048, 384], P('tok'), may hold values from -0.125 to 0.125
- up_weight: bfloat16 [64, 2048, 384], P('tok'), may hold values from -0.125 to 0.125
- down_weight: bfloat16 [64, 384, 2048], P('tok'), may hold values from -0.3125 to 0.3125
Outputs:
- layer_out: bfloat16 [4096, 2048], P(('groups', 'tok')), parts along dimension 0
There are 2 independent parts, one for each index of `groups`. A program takes and returns all parts, laid end to end along the dimension named above; an argument that names none is the same for every part. Nothing has to cross between parts.
Inputs may be any that keep to these rules, and one draw needn't show every extreme that they name: `expert_ids`: each row names 8 different experts. In each aligned block of 64 rows no expert is named by more than 12 rows; that many is reached in some block. `cache_lens`: the largest length equals 2048.
All inputs are finite; a program needn't handle non-finite values. No bound on the sum of `cache_lens` on one device may be relied on, other than what follows from the above.
Results may differ from a plain program's by a relative error of at most 0.009.
Values may be sent and summed in bfloat16 or wider, within the bound.
A program may use at most 128 MiB of HBM per device.

v0:
```python
import jax
import jax.numpy as jnp
import functools

from jax import lax
from jax.experimental import pallas as pl
from jax.experimental.pallas import tpu as pltpu
from jax.sharding import PartitionSpec as P

MESH = pl.DeviceIdType.MESH

HEADS = 32
KVH = 4
HD = 128


def head_attention(query_rows, key_rows, value_rows, allowed):

    def one_head(operands):
        query_head, key_head, value_head = operands
        scores = jnp.einsum("rgd,kd->rgk", query_head, key_head, preferred_element_type=jnp.float32)
        scores = scores * query_head.shape[-1] ** (-0.5)
        scores = jnp.where(allowed[:, None, :], scores, -1e30)
        highest = jnp.max(scores, axis=-1, keepdims=True)
        weights = jnp.exp(scores - highest)
        weights = (weights / jnp.sum(weights, axis=-1, keepdims=True)).astype(jnp.bfloat16)
        return jnp.einsum(
            "rgk,kd->rgd", weights, value_head, preferred_element_type=jnp.float32
        ).astype(jnp.bfloat16)

    return lax.map(one_head, (query_rows, key_rows, value_rows))


def place_of(count):
    place = lax.axis_index("tok")
    return place // 4, (place // 2) % 2, place % 2, count // 4


def greet(level, row, core, levels):
    barrier = pltpu.get_barrier_semaphore()

    def tell(level_to, row_to, core_to):
        pl.semaphore_signal(
            barrier,
            inc=1,
            device_id={"tok": (level_to * 2 + row_to) * 2 + core_to},
            device_id_type=MESH,
        )

    tell(level, 1 - row, core)
    tell(level, row, 1 - core)

    @pl.when(level > 0)
    def _():
        tell(level - 1, row, core)

    @pl.when(level < levels - 1)
    def _():
        tell(level + 1, row, core)

    ends = (level > 0).astype(jnp.int32) + (level < levels - 1).astype(jnp.int32)
    pl.semaphore_wait(barrier, 2 + ends)


def gather_kernel(count, rows_ref, aux_ref, all_rows, all_aux, own_sem, send_sem, recv_sem):
    level, row, core, levels = place_of(count)
    greet(level, row, core, levels)
    me = lax.axis_index("tok")

    def sends(block, way, target, first):
        out = []
        pairs = ((rows_ref, all_rows), (aux_ref, all_aux))
        for which, (own, everyone) in enumerate(pairs):
            out.append(
                pltpu.make_async_remote_copy(
                    src_ref=own if first else everyone.at[block],
                    dst_ref=everyone.at[block],
                    send_sem=send_sem.at[which, way, block],
                    recv_sem=recv_sem.at[which, block],
                    device_id={"tok": target},
                    device_id_type=MESH,
                )
            )
        return out

    def each(block, act, first=False, up=None, down=None, across=True):
        if up is not None:
            @pl.when(up)
            def _():
                for copy in sends(block, 0, me + 4, first):
                    act(copy)
        if down is not None:
            @pl.when(down)
            def _():
                for copy in sends(block, 1, me - 4, first):
                    act(copy)
        if across:
            for copy in sends(block, 2, (level * 2 + 1 - row) * 2 + core, first):
                act(copy)
        for copy in sends(block, 3, (level * 2 + row) * 2 + 1 - core, first):
            act(copy)

    def arrived(block):
        for copy in sends(block, 3, (level * 2 + row) * 2 + 1 - core, False):
            copy.wait_recv()

    start = lambda copy: copy.start()
    done = lambda copy: copy.wait_send()
    can_up, can_down = level < levels - 1, level > 0

    def line_step(distance, act, receive):
        @pl.when(level >= distance)
        def _():
            block = me - 4 * distance
            if receive:
                arrived(block)
            each(block, act, up=can_up)

        @pl.when(level + distance < levels)
        def _():
            block = me + 4 * distance
            if receive:
                arrived(block)
            each(block, act, down=can_down)

    def row_step(distance, act, receive):
        def one(level_from):
            block = (level_from * 2 + 1 - row) * 2 + core
            if receive:
                arrived(block)
            each(block, act, across=False)

        if distance == 0:
            one(level)
        else:
            @pl.when(level >= distance)
            def _():
                one(level - distance)

            @pl.when(level + distance < levels)
            def _():
                one(level + distance)

    each(me, start, first=True, up=can_up, down=can_down)
    own_rows = pltpu.make_async_copy(rows_ref, all_rows.at[me], own_sem.at[0])
    own_aux = pltpu.make_async_copy(aux_ref, all_aux.at[me], own_sem.at[1])
    own_rows.start()
    own_aux.start()
    for step in range(1, levels + 1):
        if step < levels:
            line_step(step, start, True)
        row_step(step - 1, start, True)
    for index in range(count // 2):
        arrived(index * 2 + 1 - core)
    each(me, done, first=True, up=can_up, down=can_down)
    for step in range(1, levels):
        line_step(step, done, False)
    for step in range(levels):
        row_step(step, done, False)
    own_rows.wait()
    own_aux.wait()


def gather_rows(rows, aux, count):
    anywhere = pl.BlockSpec(memory_space=pl.ANY)
    return pl.pallas_call(
        functools.partial(gather_kernel, count),
        out_shape=(
            jax.ShapeDtypeStruct((count,) + rows.shape, rows.dtype),
            jax.ShapeDtypeStruct((count,) + aux.shape, aux.dtype),
        ),
        in_specs=[anywhere, anywhere],
        out_specs=(anywhere, anywhere),
        scratch_shapes=[
            pltpu.SemaphoreType.DMA((2,)),
            pltpu.SemaphoreType.DMA((2, 4, count)),
            pltpu.SemaphoreType.DMA((2, count)),
        ],
        compiler_params=pltpu.CompilerParams(collective_id=0, has_side_effects=True),
    )(rows, aux)


def sum_kernel(
    count, parts, mixed, out, from_core, from_row, total, from_below, from_above,
    core_sem, row_sem, up_sem, down_sem,
):
    level, row, core, levels = place_of(count)
    greet(level, row, core, levels)
    me = lax.axis_index("tok")
    row_count = mixed.shape[0]
    tile = 16

    def tiles(act):
        @pl.loop(0, row_count // tile)
        def _(index):
            act(pl.ds(pl.multiple_of(index * tile, tile), tile))

    def remote(src, dst, sems, index, target):
        return pltpu.make_async_remote_copy(
            src_ref=src,
            dst_ref=dst,
            send_sem=sems.at[0, index],
            recv_sem=sems.at[1, index],
            device_id={"tok": target},
            device_id_type=MESH,
        )

    def to_core(level_to, row_to):
        slot = level_to * 2 + row_to
        target = (level * 2 + row) * 2 + 1 - core
        return remote(parts.at[slot * 2 + 1 - core], from_core.at[slot], core_sem, slot, target)

    def to_row(level_to):
        target = (level * 2 + 1 - row) * 2 + core
        slot = level_to * 2 + 1 - row
        return remote(from_core.at[slot], from_row.at[level_to], row_sem, level_to, target)

    def to_up(level_to):
        return remote(total.at[level_to], from_below.at[level_to], up_sem, level_to, me + 4)

    def to_down(level_to):
        return remote(total.at[level_to], from_above.at[level_to], down_sem, level_to, me - 4)

    def in_order(act):
        for step in range(levels - 1):
            high, low = levels - 1 - step, step

            @pl.when(high > level)
            def _():
                act(high, 1)

            @pl.when(low < level)
            def _():
                act(low, -1)

        act(level, 0)

    for row_to in (1 - row, row):
        in_order(lambda level_to, way, row_to=row_to: to_core(level_to, row_to).start())

    def pass_row(level_to, way):
        slot = level_to * 2 + 1 - row
        to_core(level_to, 1 - row).wait_recv()

        def add(where):
            both = parts[slot * 2 + core, where, :].astype(jnp.float32) + from_core[
                slot, where, :
            ].astype(jnp.float32)
            from_core[slot, where, :] = both.astype(jnp.bfloat16)

        tiles(add)
        to_row(level_to).start()

    in_order(pass_row)

    def base(slot, level_to, where):
        return (
            parts[slot * 2 + core, where, :].astype(jnp.float32)
            + from_core[slot, where, :].astype(jnp.float32)
            + from_row[level_to, where, :].astype(jnp.float32)
        )

    def pass_line(level_to, way):
        slot = level_to * 2 + row
        to_core(level_to, row).wait_recv()
        to_row(level_to).wait_recv()
        if way == 0:
            def keep(where):
                total[level_to, where, :] = base(slot, level_to, where).astype(jnp.bfloat16)

            def finish(where):
                out[where, :] = mixed[where, :] + base(slot, level_to, where)

            tiles(finish)
            for neighbour, incoming, copy in (
                (level > 0, from_below, to_up),
                (level < levels - 1, from_above, to_down),
            ):
                @pl.when(neighbour)
                def _(incoming=incoming, copy=copy):
                    copy(level_to).wait_recv()

                    def more(where):
                        out[where, :] += incoming[level_to, where, :].astype(jnp.float32)

                    tiles(more)
            return
        behind = level > 0 if way == 1 else level < levels - 1
        incoming, copy = (from_below, to_up) if way == 1 else (from_above, to_down)

        @pl.when(behind)
        def _():
            copy(level_to).wait_recv()

            def add(where):
                value = base(slot, level_to, where) + incoming[level_to, where, :].astype(
                    jnp.float32
                )
                total[level_to, where, :] = value.astype(jnp.bfloat16)

            tiles(add)

        @pl.when(jnp.logical_not(behind))
        def _():
            def add(where):
                total[level_to, where, :] = base(slot, level_to, where).astype(jnp.bfloat16)

            tiles(add)

        copy(level_to).start()

    in_order(pass_line)
    for row_to in (1 - row, row):
        in_order(lambda level_to, way, row_to=row_to: to_core(level_to, row_to).wait_send())
    in_order(lambda level_to, way: to_row(level_to).wait_send())

    def sent(level_to, way):
        if way == 1:
            to_up(level_to).wait_send()
        if way == -1:
            to_down(level_to).wait_send()

    in_order(sent)


def sum_rows(parts, mixed, count):
    row_count, width = mixed.shape
    levels = count // 4
    inside = pl.BlockSpec(memory_space=pltpu.VMEM)

    def blocks(number):
        return pltpu.VMEM((number, row_count, width), jnp.bfloat16)

    return pl.pallas_call(
        functools.partial(sum_kernel, count),
        out_shape=jax.ShapeDtypeStruct(mixed.shape, jnp.float32),
        in_specs=[inside, inside],
        out_specs=inside,
        scratch_shapes=[
            blocks(count // 2),
            blocks(levels),
            blocks(levels),
            blocks(levels),
            blocks(levels),
            pltpu.SemaphoreType.DMA((2, count // 2)),
            pltpu.SemaphoreType.DMA((2, levels)),
            pltpu.SemaphoreType.DMA((2, levels)),
            pltpu.SemaphoreType.DMA((2, levels)),
        ],
        compiler_params=pltpu.CompilerParams(
            collective_id=1, has_side_effects=True, vmem_limit_bytes=56 * 2**20
        ),
    )(parts, mixed)


def expert_kernel(
    capacity, slots, top_count, aux, rows, gate, up, down, out, picks, scale, stacked, results
):
    step = pl.program_id(0)
    experts_local = stacked.shape[0]
    groups = stacked.shape[1]
    row_count = aux.shape[2]
    block_rows = row_count // 2
    width = 2 * row_count

    @pl.when(step == 0)
    def _():
        first = (lax.axis_index("tok") * experts_local).astype(jnp.float32)
        before = lax.broadcasted_iota(jnp.int32, (width, width), 0)
        after = lax.broadcasted_iota(jnp.int32, (width, width), 1)
        earlier = ((before < after) & (before // block_rows == after // block_rows)).astype(
            jnp.bfloat16
        )
        block = (lax.broadcasted_iota(jnp.int32, (1, width), 1) // block_rows) * capacity
        slot = lax.broadcasted_iota(jnp.int32, (slots, width), 0).astype(jnp.float32)

        @pl.loop(0, groups)
        def _(group):
            both = jnp.concatenate([aux[group * 2], aux[group * 2 + 1]], axis=1)
            ids, routes = both[:top_count], both[top_count:]
            for expert in range(experts_local):
                hit = (ids == first + expert).astype(jnp.float32)
                chosen = jnp.sum(hit, axis=0, keepdims=True)
                weight = jnp.sum(hit * routes, axis=0, keepdims=True)
                rank = jnp.dot(
                    jnp.broadcast_to(chosen, (16, width)).astype(jnp.bfloat16),
                    earlier,
                    preferred_element_type=jnp.float32,
                )[:1]
                target = jnp.where(chosen > 0.5, rank + block.astype(jnp.float32), -1.0)
                pick = (slot == target).astype(jnp.float32)
                picks[group, expert * slots : (expert + 1) * slots, :] = pick.astype(jnp.bfloat16)
                scale[expert, group] = jnp.sum(pick * weight, axis=1, keepdims=True)
            source = rows[pl.ds(pl.multiple_of(group * width, width), width), :]
            taken = jnp.dot(picks[group], source, preferred_element_type=jnp.float32)
            taken = taken.astype(jnp.bfloat16)
            for expert in range(experts_local):
                stacked[expert, group] = taken[expert * slots : (expert + 1) * slots]

    depth = stacked.shape[-1]
    inputs = stacked[step].reshape(groups * slots, depth)
    gate_part = jnp.dot(inputs, gate[0], preferred_element_type=jnp.float32)
    up_part = jnp.dot(inputs, up[0], preferred_element_type=jnp.float32)
    hidden = (gate_part / (1.0 + jnp.exp(-gate_part)) * up_part).astype(jnp.bfloat16)
    result = jnp.dot(hidden, down[0], preferred_element_type=jnp.float32)
    result = result * scale[step].reshape(groups * slots, 1)
    results[step] = result.astype(jnp.bfloat16).reshape(groups, slots, depth)

    @pl.when(step == experts_local - 1)
    def _():
        @pl.loop(0, groups)
        def _(group):
            value = jnp.concatenate([results[e, group] for e in range(experts_local)], axis=0)
            summed = lax.dot_general(
                picks[group], value, (((0,), (0,)), ((), ())), preferred_element_type=jnp.float32
            )
            out[pl.ds(pl.multiple_of(group * width, width), width), :] = summed.astype(
                jnp.bfloat16
            )


def run_experts(aux, rows, gate_weight, up_weight, down_weight, capacity):
    count, doubled, row_count = aux.shape
    experts_local, depth, hidden = gate_weight.shape
    groups = count // 2
    slots = -(-4 * capacity // 16) * 16
    whole = dict(pipeline_mode=pl.Buffered(1))
    return pl.pallas_call(
        functools.partial(expert_kernel, capacity, slots, doubled // 2),
        grid=(experts_local,),
        out_shape=jax.ShapeDtypeStruct(rows.shape, jnp.bfloat16),
        in_specs=[
            pl.BlockSpec(aux.shape, lambda e: (0, 0, 0), **whole),
            pl.BlockSpec(rows.shape, lambda e: (0, 0), **whole),
            pl.BlockSpec((1, depth, hidden), lambda e: (e, 0, 0)),
            pl.BlockSpec((1, depth, hidden), lambda e: (e, 0, 0)),
            pl.BlockSpec((1, hidden, depth), lambda e: (e, 0, 0)),
        ],
        out_specs=pl.BlockSpec(rows.shape, lambda e: (0, 0), **whole),
        scratch_shapes=[
            pltpu.VMEM((groups, experts_local * slots, 2 * row_count), jnp.bfloat16),
            pltpu.VMEM((experts_local, groups, slots, 1), jnp.float32),
            pltpu.VMEM((experts_local, groups, slots, depth), jnp.bfloat16),
            pltpu.VMEM((experts_local, groups, slots, depth), jnp.bfloat16),
        ],
        compiler_params=pltpu.CompilerParams(
            dimension_semantics=("arbitrary",), vmem_limit_bytes=62 * 2**20
        ),
    )(aux, rows, gate_weight, up_weight, down_weight)


def body(
    queries,
    new_keys,
    new_values,
    cache_keys,
    cache_values,
    cache_lens,
    residual,
    out_weight,
    norm_gain,
    expert_ids,
    route_weights,
    gate_weight,
    up_weight,
    down_weight,
):
    devices = lax.axis_size("tok")
    group = HEADS // KVH
    row_count = residual.shape[0]
    block_rows = row_count // 2
    top_count = expert_ids.shape[1]
    experts_local = gate_weight.shape[0]
    experts_all = experts_local * devices
    capacity = max(2, block_rows * top_count * 3 // (2 * experts_all))
    cache_rows = cache_keys.shape[0]
    length = cache_lens[0]
    key_all = jnp.concatenate([cache_keys, new_keys], 0).reshape(-1, KVH, HD).transpose(1, 0, 2)
    value_all = (
        jnp.concatenate([cache_values, new_values], 0).reshape(-1, KVH, HD).transpose(1, 0, 2)
    )
    place = lax.axis_index("tok")
    core = place % 2
    same_core = [list(range(parity, devices, 2)) for parity in range(2)]
    swap = [(i, i ^ 1) for i in range(devices)]
    core_weight = lax.all_gather(
        out_weight, "tok", axis=0, tiled=True, axis_index_groups=same_core
    )
    positions = jnp.arange(row_count)
    cache_ok = jnp.broadcast_to(jnp.arange(cache_rows)[None, :] < length, (row_count, cache_rows))
    new_ok = jnp.arange(new_keys.shape[0])[None, :] <= positions[:, None]
    allowed = jnp.concatenate([cache_ok, new_ok], 1)
    shaped = queries.reshape(row_count, KVH, group, HD).transpose(1, 0, 2, 3)
    output = head_attention(shaped, key_all, value_all, allowed)
    attended = output.transpose(1, 0, 2, 3).reshape(row_count, devices // 2, 2, -1)
    own_columns = lax.dynamic_index_in_dim(attended, core, 2, keepdims=False)
    other_columns = lax.dynamic_index_in_dim(attended, 1 - core, 2, keepdims=False)
    own_columns = own_columns.reshape(row_count, -1)
    other_columns = other_columns.reshape(row_count, -1)
    sibling_rows = lax.ppermute(other_columns, "tok", swap)
    for_sibling = jnp.dot(
        sibling_rows, core_weight, preferred_element_type=jnp.float32
    ).astype(jnp.bfloat16)
    from_sibling = lax.ppermute(for_sibling, "tok", swap)
    own_part = jnp.dot(own_columns, core_weight, preferred_element_type=jnp.float32)
    mixed = residual.astype(jnp.float32) + own_part + from_sibling.astype(jnp.float32)
    factor = lax.rsqrt(jnp.mean(mixed * mixed, axis=-1, keepdims=True) + 1e-06)
    normed = (mixed * factor * norm_gain).astype(jnp.bfloat16)
    aux = jnp.concatenate([expert_ids.astype(jnp.float32).T, route_weights.T], axis=0)
    all_rows, all_aux = gather_rows(normed, aux, devices)
    summed = run_experts(
        all_aux,
        all_rows.reshape(devices * row_count, -1),
        gate_weight,
        up_weight,
        down_weight,
        capacity,
    )
    final = sum_rows(summed.reshape(devices, row_count, -1), mixed, devices)
    return final.astype(jnp.bfloat16)


def solution(mesh):
    placed = (
        P(("groups", "tok"), None),
        P(("groups", "tok"), None),
        P(("groups", "tok"), None),
        P(("groups", "tok"), None),
        P(("groups", "tok"), None),
        P(("groups", "tok")),
        P(("groups", "tok"), None),
        P("tok", None),
        P(),
        P(("groups", "tok"), None),
        P(("groups", "tok"), None),
        P("tok", None, None),
        P("tok", None, None),
        P("tok", None, None),
    )
    return jax.shard_map(
        body, mesh=mesh, in_specs=placed, out_specs=P(("groups", "tok"), None), check_vma=False
    )
```

profile of v0, /device:TPU:13, one launch (start us, length us, event | category | flops | bytes accessed | tf_op | source)
XLA Modules:
  0.0 301.0 jit_solution(15992364994361811514)
XLA Ops:
  9.0 1.0 copy.19
  10.0 1.6 copy.15
  11.6 2.5 copy.16
  14.1 2.9 copy.18
  17.1 3.3 %pad_maximum_fusion = bf16[2176,512]{0,1:T(8,128)(2,1)} fusion(bf16[128,512]{0,1:T(8,128)(2,1)S(1)} %copy.17, bf16[2048,512]{0,1:T(8,128)(2,1)} %copy.16), kind=kLoop, calls=%fused_computation.34 | loop fusion | flops 4456448 | bytes 4456448 | tf_op jit(solution)/shard_map/concatenate | solution.py:478
  20.4 1.7 pad_maximum_fusion.1
  22.1 49.0 %while.10 = (s32[]{:T(128)}, bf16[4,128,8,128]{1,3,2,0:T(8,128)(2,1)}, pred[128,2176]{1,0:T(8,128)(4,1)S(1)}, bf16[4,128,8,128]{1,3,2,0:T(8,128)(2,1)S(1)}, bf16...) while((s32[]{:T(128)}, bf16[4,128,8,128]{1,3,2,0:T(8,128)(2,1)}, ...), condition=%wide.region_3.4_spmd, body=%wide.region_0.3_spmd.sunk | while | flops 1731466496 | bytes 4074073 | solution.py:31
  22.2 4.6 %fusion.69 = f32[128,8]{0,1:T(8,128)S(1)} fusion(pred[128,2176]{1,0:T(8,128)(4,1)S(1)} %get-tuple-element.117, bf16[4,2176,128]{1,2,0:T(8,128)(2,1)} %get-tuple-element.119, s32[]{:T(128)S(6)} %copy.34, bf16[4,128,8,128]{1,3,2,0:T(8,128)(2,1)S(1)} %get-tuple-element.118), kind=kOutput, calls=%fused_computation.47.clone.1 | convolution fusion | flops 579340416 | bytes 1102848 | tf_op jit(solution)/shard_map/while/body/eval_jaxpr/sub | solution.py:25
  26.8 6.7 %fusion.70 = bf16[1,128,8,128]{3,1,2,0:T(8,128)(2,1)S(1)} fusion(f32[128,8]{0,1:T(8,128)S(1)} %fusion.69, bf16[4,2176,128]{1,2,0:T(8,128)(2,1)} %get-tuple-element.120, s32[]{:T(128)S(6)} %copy.34, pred[128,2176]{1,0:T(8,128)(4,1)S(1)} %get-tuple-element.117, bf16[4,2176,128]{1,2,0:T(8,128)(2,1)} %get-tuple-element.119, ...), kind=kOutput, calls=%fused_computation.11.clone.1 | convolution fusion | flops 1152126080 | bytes 1922560 | tf_op jit(solution)/shard_map/while/body/eval_jaxpr/rgk,kd->rgd/dot_general | solution.py:27
  34.4 4.6 %fusion.69 = f32[128,8]{0,1:T(8,128)S(1)} fusion(pred[128,2176]{1,0:T(8,128)(4,1)S(1)} %get-tuple-element.117, bf16[4,2176,128]{1,2,0:T(8,128)(2,1)} %get-tuple-element.119, s32[]{:T(128)S(6)} %copy.34, bf16[4,128,8,128]{1,3,2,0:T(8,128)(2,1)S(1)} %get-tuple-element.118), kind=kOutput, calls=%fused_computation.47.clone.1 | convolution fusion | flops 579340416 | bytes 1102848 | tf_op jit(solution)/shard_map/while/body/eval_jaxpr/sub | solution.py:25
  39.0 6.7 %fusion.70 = bf16[1,128,8,128]{3,1,2,0:T(8,128)(2,1)S(1)} fusion(f32[128,8]{0,1:T(8,128)S(1)} %fusion.69, bf16[4,2176,128]{1,2,0:T(8,128)(2,1)} %get-tuple-element.120, s32[]{:T(128)S(6)} %copy.34, pred[128,2176]{1,0:T(8,128)(4,1)S(1)} %get-tuple-element.117, bf16[4,2176,128]{1,2,0:T(8,128)(2,1)} %get-tuple-element.119, ...), kind=kOutput, calls=%fused_computation.11.clone.1 | convolution fusion | flops 1152126080 | bytes 1922560 | tf_op jit(solution)/shard_map/while/body/eval_jaxpr/rgk,kd->rgd/dot_general | solution.py:27
  46.6 4.6 %fusion.69 = f32[128,8]{0,1:T(8,128)S(1)} fusion(pred[128,2176]{1,0:T(8,128)(4,1)S(1)} %get-tuple-element.117, bf16[4,2176,128]{1,2,0:T(8,128)(2,1)} %get-tuple-element.119, s32[]{:T(128)S(6)} %copy.34, bf16[4,128,8,128]{1,3,2,0:T(8,128)(2,1)S(1)} %get-tuple-element.118), kind=kOutput, calls=%fused_computation.47.clone.1 | convolution fusion | flops 579340416 | bytes 1102848 | tf_op jit(solution)/shard_map/while/body/eval_jaxpr/sub | solution.py:25
  51.2 6.7 %fusion.70 = bf16[1,128,8,128]{3,1,2,0:T(8,128)(2,1)S(1)} fusion(f32[128,8]{0,1:T(8,128)S(1)} %fusion.69, bf16[4,2176,128]{1,2,0:T(8,128)(2,1)} %get-tuple-element.120, s32[]{:T(128)S(6)} %copy.34, pred[128,2176]{1,0:T(8,128)(4,1)S(1)} %get-tuple-element.117, bf16[4,2176,128]{1,2,0:T(8,128)(2,1)} %get-tuple-element.119, ...), kind=kOutput, calls=%fused_computation.11.clone.1 | convolution fusion | flops 1152126080 | bytes 1922560 | tf_op jit(solution)/shard_map/while/body/eval_jaxpr/rgk,kd->rgd/dot_general | solution.py:27
  58.8 4.6 %fusion.69 = f32[128,8]{0,1:T(8,128)S(1)} fusion(pred[128,2176]{1,0:T(8,128)(4,1)S(1)} %get-tuple-element.117, bf16[4,2176,128]{1,2,0:T(8,128)(2,1)} %get-tuple-element.119, s32[]{:T(128)S(6)} %copy.34, bf16[4,128,8,128]{1,3,2,0:T(8,128)(2,1)S(1)} %get-tuple-element.118), kind=kOutput, calls=%fused_computation.47.clone.1 | convolution fusion | flops 579340416 | bytes 1102848 | tf_op jit(solution)/shard_map/while/body/eval_jaxpr/sub | solution.py:25
  63.4 6.8 %fusion.70 = bf16[1,128,8,128]{3,1,2,0:T(8,128)(2,1)S(1)} fusion(f32[128,8]{0,1:T(8,128)S(1)} %fusion.69, bf16[4,2176,128]{1,2,0:T(8,128)(2,1)} %get-tuple-element.120, s32[]{:T(128)S(6)} %copy.34, pred[128,2176]{1,0:T(8,128)(4,1)S(1)} %get-tuple-element.117, bf16[4,2176,128]{1,2,0:T(8,128)(2,1)} %get-tuple-element.119, ...), kind=kOutput, calls=%fused_computation.11.clone.1 | convolution fusion | flops 1152126080 | bytes 1922560 | tf_op jit(solution)/shard_map/while/body/eval_jaxpr/rgk,kd->rgd/dot_general | solution.py:27
  71.2 1.3 constant_dynamic-slice_fusion
  74.8 57.7 %all-gather.2.cloned.1.call-done = bf16[2048,2048]{1,0:T(8,128)(2,1)} async-done(((bf16[256,2048]{1,0:T(8,128)(2,1)}), bf16[2048,2048]{1,0:T(8,128)(2,1)}) %all-gather.2.cloned.1.call-update) | async-done | bytes 8388624 | tf_op jit(solution)/shard_map/all_gather | solution.py:486
  132.5 4.8 %convolution_convert_fusion = bf16[128,2048]{1,0:T(8,128)(2,1)S(1)} fusion(bf16[128,2048]{0,1:T(8,128)(2,1)S(1)} %collective-permute-done, bf16[2048,2048]{1,0:T(8,128)(2,1)} %all-gather.2.cloned.1.call-done), kind=kOutput, calls=%fused_computation.33 | convolution fusion | flops 1074003968 | bytes 9437184 | tf_op jit(solution)/shard_map/dot_general | solution.py:501
  138.3 1.3 convolution_add_fusion
  140.1 1.1 multiply_convert_fusion.rows_ref
  141.2 55.8 %shard_map.136 = (bf16[16,128,2048]{2,1,0:T(8,128)(2,1)}, f32[16,16,128]{2,1,0:T(8,128)}) custom-call(bf16[128,2048]{1,0:T(8,128)(2,1)} %multiply_convert_fusion.rows_ref, f32[16,128]{1,0:T(8,128)} %pad_maximum_fusion.2.aux_ref), custom_call_target="tpu_custom_call" | custom-call | tf_op jit(solution)/shard_map/pallas_call | solution.py:166
  197.0 27.1 %shard_map.137 = bf16[2048,2048]{1,0:T(8,128)(2,1)} custom-call(f32[16,16,128]{2,1,0:T(8,128)} %get-tuple-element.40.aux, bf16[2048,2048]{1,0:T(8,128)(2,1)} %bitcast.74, bf16[4,2048,384]{2,1,0:T(8,128)(2,1)} %gate.1, bf16[4,2048,384]{2,1,0:T(8,128)(2,1)} %up.1, bf16[4,384,2048]{2,1,0:T(8,128)(2,1)} %down.1), custom_call_target="tpu_custom_call" | custom-call | tf_op jit(solution)/shard_map/pallas_call | solution.py:428
  224.2 67.9 %shard_map.138 = f32[128,2048]{1,0:T(8,128)} custom-call(bf16[16,128,2048]{2,1,0:T(8,128)(2,1)} %bitcast.73, f32[128,2048]{1,0:T(8,128)} %copy-done.1), custom_call_target="tpu_custom_call" | custom-call | tf_op jit(solution)/shard_map/pallas_call | solution.py:334
  292.1 2.1 convert_element_type.29
  (38 shorter events, 9.3 us)
Async XLA Ops:
  6.5 5.1 %copy-start.2 = (bf16[2048,512]{1,0:T(8,128)(2,1)S(1)}, bf16[2048,512]{1,0:T(8,128)(2,1)}, u32[]{:S(2)}) copy-start(bf16[2048,512]{1,0:T(8,128)(2,1)} %param.19) | copy-start | bytes 6291460
  6.5 126.0 %all-gather.2.cloned.1.call-start = ((), (), s32[]{:S(2)}) async-start(), calls=%async_computation | async-start | bytes 9437184 | tf_op jit(solution)/shard_map/all_gather | solution.py:486
  22.1 51.1 %copy-start.5 = (s32[128,8]{0,1:T(8,128)S(1)}, s32[128,8]{0,1:T(8,128)}, u32[]{:S(2)}) copy-start(s32[128,8]{0,1:T(8,128)} %param.25) | copy-start | bytes 12292
  22.1 51.1 %copy-start.6 = (f32[128,8]{0,1:T(8,128)S(1)}, f32[128,8]{0,1:T(8,128)}, u32[]{:S(2)}) copy-start(f32[128,8]{0,1:T(8,128)} %param.26) | copy-start | bytes 12292
  72.4 2.4 collective-permute-start
  73.9 64.4 %copy-start.3 = (bf16[128,2048]{1,0:T(8,128)(2,1)S(1)}, bf16[128,2048]{1,0:T(8,128)(2,1)}, u32[]{:S(2)}) copy-start(bf16[128,2048]{1,0:T(8,128)(2,1)} %param.22) | copy-start | bytes 1572868
  132.5 5.8 %copy-start = (bf16[2048,2048]{1,0:T(8,128)(2,1)S(1)}, bf16[2048,2048]{1,0:T(8,128)(2,1)}, u32[]{:S(2)}) copy-start(bf16[2048,2048]{1,0:T(8,128)(2,1)} %all-gather.2.cloned.1.call-done) | copy-start | bytes 25165828
  137.3 2.5 collective-permute-start.1
  138.3 1.8 copy-start.4
  140.1 84.1 %copy-start.1 = (f32[128,2048]{1,0:T(8,128)}, f32[128,2048]{1,0:T(8,128)S(1)}, u32[]{:S(2)}) copy-start(f32[128,2048]{1,0:T(8,128)S(1)} %get-tuple-element.61.mixed) | copy-start | bytes 3145732
Sparse Core Ops, SparseCore 0:
  9.5 122.9 all-gather.1
where the time goes:
time: 306 us; the launch traced here: 301 us
  Pallas kernels  151 us (49%)
  waiting for transfers between devices  59.6 us (19%)
  matrix products  51.4 us (17%)
  between operations  14.2 us (5%)
  local copies, waits for them, and re-layouts  14 us (5%)
  other arithmetic  9.09 us (3%)
    pallas_call x1, Pallas kernels, sum_rows(): pl.pallas_call(functools.partial(sum_kernel, count), out_shape=jax.ShapeD...  67.9 us
    all_gather x1, waiting for transfers between devices, body(): lax.all_gather(out_weight, 'tok', axis=0, tiled=True, axis_index_groups=s...  57.7 us
    pallas_call x1, Pallas kernels, gather_rows(): pl.pallas_call(functools.partial(gather_kernel, count), out_shape=(jax.Sh...  55.8 us
    pallas_call x1, Pallas kernels, run_experts(): pl.pallas_call(functools.partial(expert_kernel, capacity, slots, doubled...  27.1 us
    dot_general x4, matrix products, one_head(): jnp.einsum('rgk,kd->rgd', weights, value_head, preferred_element_type=jnp...  26.9 us
    sub x4, matrix products, one_head(): weights = jnp.exp(scores - highest)  18.4 us
    unnamed x19, local copies, waits for them, and re-layouts  9.09 us
  transfers between devices with their start and end apart: 3, of which 3 were waited for; matrix products, arithmetic and copies ran while one was open for 22% of the time, Pallas kernels for 0%

commit v1 on v0

--- a/solution.py
+++ b/solution.py
@@ -483,8 +483,12 @@
     core = place % 2
     same_core = [list(range(parity, devices, 2)) for parity in range(2)]
     swap = [(i, i ^ 1) for i in range(devices)]
+    groups = lax.axis_size("groups")
+    part = lax.axis_index("groups")
+    piece_rows = out_weight.shape[0] // groups
+    piece = lax.dynamic_slice_in_dim(out_weight, part * piece_rows, piece_rows, 0)
     core_weight = lax.all_gather(
-        out_weight, "tok", axis=0, tiled=True, axis_index_groups=same_core
+        piece, "tok", axis=0, tiled=True, axis_index_groups=same_core
     )
     positions = jnp.arange(row_count)
     cache_ok = jnp.broadcast_to(jnp.arange(cache_rows)[None, :] < length, (row_count, cache_rows))
@@ -492,18 +496,31 @@
     allowed = jnp.concatenate([cache_ok, new_ok], 1)
     shaped = queries.reshape(row_count, KVH, group, HD).transpose(1, 0, 2, 3)
     output = head_attention(shaped, key_all, value_all, allowed)
-    attended = output.transpose(1, 0, 2, 3).reshape(row_count, devices // 2, 2, -1)
+    attended = output.transpose(1, 0, 2, 3).reshape(
+        row_count, devices // 2, 2, groups, piece_rows
+    )
     own_columns = lax.dynamic_index_in_dim(attended, core, 2, keepdims=False)
     other_columns = lax.dynamic_index_in_dim(attended, 1 - core, 2, keepdims=False)
-    own_columns = own_columns.reshape(row_count, -1)
-    other_columns = other_columns.reshape(row_count, -1)
-    sibling_rows = lax.ppermute(other_columns, "tok", swap)
-    for_sibling = jnp.dot(
-        sibling_rows, core_weight, preferred_element_type=jnp.float32
-    ).astype(jnp.bfloat16)
-    from_sibling = lax.ppermute(for_sibling, "tok", swap)
-    own_part = jnp.dot(own_columns, core_weight, preferred_element_type=jnp.float32)
-    mixed = residual.astype(jnp.float32) + own_part + from_sibling.astype(jnp.float32)
+    sibling_columns = lax.ppermute(other_columns, "tok", swap)
+    both = jnp.concatenate([own_columns, sibling_columns], 0)
+    projected = []
+    for step in range(groups):
+        rows = lax.dynamic_index_in_dim(both, (part + step) % groups, 2, keepdims=False)
+        rows = rows.reshape(2 * row_count, -1)
+        if step:
+            ahead = [(i, (i + step) % groups) for i in range(groups)]
+            rows = lax.ppermute(rows, "groups", ahead)
+        projected.append(jnp.dot(rows, core_weight, preferred_element_type=jnp.float32))
+    mixed = residual.astype(jnp.float32)
+    for step in reversed(range(groups)):
+        from_sibling = lax.ppermute(
+            projected[step][row_count:].astype(jnp.bfloat16), "tok", swap
+        )
+        summed_rows = projected[step][:row_count] + from_sibling.astype(jnp.float32)
+        if step:
+            back = [(i, (i - step) % groups) for i in range(groups)]
+            summed_rows = lax.ppermute(summed_rows.astype(jnp.bfloat16), "groups", back)
+        mixed = mixed + summed_rows.astype(jnp.float32)
     factor = lax.rsqrt(jnp.mean(mixed * mixed, axis=-1, keepdims=True) + 1e-06)
     normed = (mixed * factor * norm_gain).astype(jnp.bfloat16)
     aux = jnp.concatenate([expert_ids.astype(jnp.float32).T, route_weights.T], axis=0)

time: 306 us -> 276 us (0.902)
  waiting for transfers between devices: 59.6 us -> 24.5 us
    all_gather x1, waiting for transfers between devices: 57.7 us -> 0.01 us  [body(): lax.all_gather(piece, 'tok', axis=0, tiled=True, axis_index_groups=same_c...]
    ppermute x2 -> x5, waiting for transfers between devices: 1.16 us -> 24.5 us  [the longest x1 11.9 us: body(): rows = lax.ppermute(rows, 'groups', ahead)]
    dynamic_update_slice x8 -> x0, local copies, waits for them, and re-layouts: 3.68 us -> none  [head_attention(): return lax.map(one_head, (query_rows, key_rows, value_rows))]
    pallas_call x1, Pallas kernels: 67.9 us -> 71.5 us  [sum_rows(): pl.pallas_call(functools.partial(sum_kernel, count), out_shape=jax.ShapeD...]
    pallas_call x1, Pallas kernels: 55.8 us -> 52.4 us  [gather_rows(): pl.pallas_call(functools.partial(gather_kernel, count), out_shape=(jax.Sh...]
    unnamed x19 -> x25, local copies, waits for them, and re-layouts: 9.09 us -> 11.9 us
  transfers between devices with their start and end apart: 3 -> 6, of which waited for: 3 -> 4; matrix products, arithmetic and copies ran while one was open for 22% -> 24% of each run, Pallas kernels for 0% -> 0%
where the time goes in v1:
time: 276 us; the launch traced here: 271 us
  Pallas kernels  151 us (55%)
  matrix products  52.9 us (19%)
  waiting for transfers between devices  24.5 us (9%)
  between operations  14.3 us (5%)
  local copies, waits for them, and re-layouts  14.2 us (5%)
  other arithmetic  9.32 us (3%)
  starting transfers between devices  4.63 us (2%)
    pallas_call x1, Pallas kernels, sum_rows(): pl.pallas_call(functools.partial(sum_kernel, count), out_shape=jax.ShapeD...  71.5 us
    pallas_call x1, Pallas kernels, gather_rows(): pl.pallas_call(functools.partial(gather_kernel, count), out_shape=(jax.Sh...  52.4 us
    dot_general x4, matrix products, one_head(): jnp.einsum('rgk,kd->rgd', weights, value_head, preferred_element_type=jnp...  29.6 us
    pallas_call x1, Pallas kernels, run_experts(): pl.pallas_call(functools.partial(expert_kernel, capacity, slots, doubled...  27 us
    sub x4, matrix products, one_head(): weights = jnp.exp(scores - highest)  18.4 us
    ppermute x1, waiting for transfers between devices, body(): rows = lax.ppermute(rows, 'groups', ahead)  11.9 us
    unnamed x25, local copies, waits for them, and re-layouts  11.9 us
    ppermute x1, waiting for transfers between devices, body(): summed_rows = lax.ppermute(summed_rows.astype(jnp.bfloat16), 'groups', back)  11.3 us
  transfers between devices with their start and end apart: 6, of which 4 were waited for; matrix products, arithmetic and copies ran while one was open for 24% of the time, Pallas kernels for 0%

profile of v1, /device:TPU:13, one launch (start us, length us, event | category | flops | bytes accessed | tf_op | source)
XLA Modules:
  0.0 270.9 jit_solution(17199410274274221644)
XLA Ops:
  11.4 1.6 copy.15
  13.0 2.5 copy.16
  15.5 2.9 %copy.18 = bf16[2048,512]{0,1:T(8,128)(2,1)S(1)} copy(bf16[2048,512]{1,0:T(8,128)(2,1)} %param.20) | data formatting | bytes 4194304 | tf_op args[4]
  18.5 3.3 %pad_maximum_fusion = bf16[2176,512]{0,1:T(8,128)(2,1)} fusion(bf16[128,512]{0,1:T(8,128)(2,1)S(1)} %copy.17, bf16[2048,512]{0,1:T(8,128)(2,1)} %copy.16), kind=kLoop, calls=%fused_computation.32 | loop fusion | flops 4456448 | bytes 4456448 | tf_op jit(solution)/shard_map/concatenate | solution.py:478
  21.9 1.6 pad_maximum_fusion.1
  23.6 48.1 %while.10 = (s32[]{:T(128)}, bf16[4,128,8,128]{3,1,2,0:T(8,128)(2,1)}, pred[128,2176]{1,0:T(8,128)(4,1)S(1)}, bf16[4,128,8,128]{1,3,2,0:T(8,128)(2,1)S(1)}, bf16...) while((s32[]{:T(128)}, bf16[4,128,8,128]{3,1,2,0:T(8,128)(2,1)}, ...), condition=%wide.region_3.4_spmd, body=%wide.region_0.3_spmd.sunk | while | flops 1731466496 | bytes 3026005 | solution.py:31
  23.6 4.6 %fusion.77 = f32[128,8]{0,1:T(8,128)S(1)} fusion(pred[128,2176]{1,0:T(8,128)(4,1)S(1)} %get-tuple-element.119, bf16[4,2176,128]{1,2,0:T(8,128)(2,1)} %get-tuple-element.121, s32[]{:T(128)S(6)} %copy.33, bf16[4,128,8,128]{1,3,2,0:T(8,128)(2,1)S(1)} %get-tuple-element.120), kind=kOutput, calls=%fused_computation.57.clone.1 | convolution fusion | flops 579340416 | bytes 1102848 | tf_op jit(solution)/shard_map/while/body/eval_jaxpr/sub | solution.py:25
  28.2 7.4 %fusion.78 = bf16[4,128,8,128]{3,1,2,0:T(8,128)(2,1)} fusion(bf16[4,128,8,128]{3,1,2,0:T(8,128)(2,1)} %get-tuple-element.111, s32[]{:T(128)S(6)} %copy.33, f32[128,8]{0,1:T(8,128)S(1)} %fusion.77, bf16[4,2176,128]{1,2,0:T(8,128)(2,1)} %get-tuple-element.122, pred[128,2176]{1,0:T(8,128)(4,1)S(1)} %get-tuple-element.119, ...), kind=kOutput, calls=%fused_computation.12.clone.1 | convolution fusion | flops 1152126080 | bytes 1923072 | tf_op jit(solution)/shard_map/while/body/eval_jaxpr/rgk,kd->rgd/dot_general | solution.py:27
  35.6 4.6 %fusion.77 = f32[128,8]{0,1:T(8,128)S(1)} fusion(pred[128,2176]{1,0:T(8,128)(4,1)S(1)} %get-tuple-element.119, bf16[4,2176,128]{1,2,0:T(8,128)(2,1)} %get-tuple-element.121, s32[]{:T(128)S(6)} %copy.33, bf16[4,128,8,128]{1,3,2,0:T(8,128)(2,1)S(1)} %get-tuple-element.120), kind=kOutput, calls=%fused_computation.57.clone.1 | convolution fusion | flops 579340416 | bytes 1102848 | tf_op jit(solution)/shard_map/while/body/eval_jaxpr/sub | solution.py:25
  40.2 7.4 %fusion.78 = bf16[4,128,8,128]{3,1,2,0:T(8,128)(2,1)} fusion(bf16[4,128,8,128]{3,1,2,0:T(8,128)(2,1)} %get-tuple-element.111, s32[]{:T(128)S(6)} %copy.33, f32[128,8]{0,1:T(8,128)S(1)} %fusion.77, bf16[4,2176,128]{1,2,0:T(8,128)(2,1)} %get-tuple-element.122, pred[128,2176]{1,0:T(8,128)(4,1)S(1)} %get-tuple-element.119, ...), kind=kOutput, calls=%fused_computation.12.clone.1 | convolution fusion | flops 1152126080 | bytes 1923072 | tf_op jit(solution)/shard_map/while/body/eval_jaxpr/rgk,kd->rgd/dot_general | solution.py:27
  47.6 4.6 %fusion.77 = f32[128,8]{0,1:T(8,128)S(1)} fusion(pred[128,2176]{1,0:T(8,128)(4,1)S(1)} %get-tuple-element.119, bf16[4,2176,128]{1,2,0:T(8,128)(2,1)} %get-tuple-element.121, s32[]{:T(128)S(6)} %copy.33, bf16[4,128,8,128]{1,3,2,0:T(8,128)(2,1)S(1)} %get-tuple-element.120), kind=kOutput, calls=%fused_computation.57.clone.1 | convolution fusion | flops 579340416 | bytes 1102848 | tf_op jit(solution)/shard_map/while/body/eval_jaxpr/sub | solution.py:25
  52.2 7.4 %fusion.78 = bf16[4,128,8,128]{3,1,2,0:T(8,128)(2,1)} fusion(bf16[4,128,8,128]{3,1,2,0:T(8,128)(2,1)} %get-tuple-element.111, s32[]{:T(128)S(6)} %copy.33, f32[128,8]{0,1:T(8,128)S(1)} %fusion.77, bf16[4,2176,128]{1,2,0:T(8,128)(2,1)} %get-tuple-element.122, pred[128,2176]{1,0:T(8,128)(4,1)S(1)} %get-tuple-element.119, ...), kind=kOutput, calls=%fused_computation.12.clone.1 | convolution fusion | flops 1152126080 | bytes 1923072 | tf_op jit(solution)/shard_map/while/body/eval_jaxpr/rgk,kd->rgd/dot_general | solution.py:27
  59.6 4.6 %fusion.77 = f32[128,8]{0,1:T(8,128)S(1)} fusion(pred[128,2176]{1,0:T(8,128)(4,1)S(1)} %get-tuple-element.119, bf16[4,2176,128]{1,2,0:T(8,128)(2,1)} %get-tuple-element.121, s32[]{:T(128)S(6)} %copy.33, bf16[4,128,8,128]{1,3,2,0:T(8,128)(2,1)S(1)} %get-tuple-element.120), kind=kOutput, calls=%fused_computation.57.clone.1 | convolution fusion | flops 579340416 | bytes 1102848 | tf_op jit(solution)/shard_map/while/body/eval_jaxpr/sub | solution.py:25
  64.2 7.4 %fusion.78 = bf16[4,128,8,128]{3,1,2,0:T(8,128)(2,1)} fusion(bf16[4,128,8,128]{3,1,2,0:T(8,128)(2,1)} %get-tuple-element.111, s32[]{:T(128)S(6)} %copy.33, f32[128,8]{0,1:T(8,128)S(1)} %fusion.77, bf16[4,2176,128]{1,2,0:T(8,128)(2,1)} %get-tuple-element.122, pred[128,2176]{1,0:T(8,128)(4,1)S(1)} %get-tuple-element.119, ...), kind=kOutput, calls=%fused_computation.12.clone.1 | convolution fusion | flops 1152126080 | bytes 1923072 | tf_op jit(solution)/shard_map/while/body/eval_jaxpr/rgk,kd->rgd/dot_general | solution.py:27
  71.6 1.3 constant_dynamic-slice_fusion.1
  76.9 11.9 %collective-permute-done.1 = bf16[256,1024]{0,1:T(8,128)(2,1)S(1)} collective-permute-done((bf16[256,1024]{0,1:T(8,128)(2,1)S(1)}, bf16[256,1024]{0,1:T(8,128)(2,1)S(1)}, u32[]{:S(2)}, u32[]{:S(2)}) %collective-permute-start.1) | collective-permute-done | bytes 524320 | tf_op jit(solution)/shard_map/ppermute | solution.py:512
  88.8 3.6 %fusion.59 = f32[256,2048]{1,0:T(8,128)S(1)} fusion(bf16[256,1024]{0,1:T(8,128)(2,1)S(1)} %collective-permute-done.1, bf16[1024,2048]{1,0:T(8,128)(2,1)} %all-gather.2.cloned.1.call-done), kind=kOutput, calls=%fused_computation.58 | convolution fusion | flops 1073741824 | bytes 6815744 | tf_op jit(solution)/shard_map/dot_general | solution.py:513
  92.5 1.3 collective-permute-start.2
  93.8 1.3 fusion.60
  97.3 11.3 %collective-permute-done.3 = bf16[128,2048]{1,0:T(8,128)(2,1)S(1)} collective-permute-done((bf16[128,2048]{1,0:T(8,128)(2,1)S(1)}, bf16[128,2048]{1,0:T(8,128)(2,1)S(1)}, u32[]{:S(2)}, u32[]{:S(2)}) %collective-permute-start.3) | collective-permute-done | bytes 524320 | tf_op jit(solution)/shard_map/ppermute | solution.py:522
  110.9 52.4 %shard_map.136 = (bf16[16,128,2048]{2,1,0:T(8,128)(2,1)}, f32[16,16,128]{2,1,0:T(8,128)}) custom-call(bf16[128,2048]{1,0:T(8,128)(2,1)} %multiply_convert_fusion.rows_ref, f32[16,128]{1,0:T(8,128)} %pad_maximum_fusion.2.aux_ref), custom_call_target="tpu_custom_call" | custom-call | tf_op jit(solution)/shard_map/pallas_call | solution.py:166
  163.4 27.0 %shard_map.137 = bf16[2048,2048]{1,0:T(8,128)(2,1)} custom-call(f32[16,16,128]{2,1,0:T(8,128)} %get-tuple-element.40.aux, bf16[2048,2048]{1,0:T(8,128)(2,1)} %bitcast.78, bf16[4,2048,384]{2,1,0:T(8,128)(2,1)} %gate.1, bf16[4,2048,384]{2,1,0:T(8,128)(2,1)} %up.1, bf16[4,384,2048]{2,1,0:T(8,128)(2,1)} %down.1), custom_call_target="tpu_custom_call" | custom-call | tf_op jit(solution)/shard_map/pallas_call | solution.py:428
  190.4 71.5 %shard_map.138 = f32[128,2048]{1,0:T(8,128)} custom-call(bf16[16,128,2048]{2,1,0:T(8,128)(2,1)} %bitcast.77, f32[128,2048]{1,0:T(8,128)} %copy-done.2), custom_call_target="tpu_custom_call" | custom-call | tf_op jit(solution)/shard_map/pallas_call | solution.py:334
  262.0 2.1 convert_element_type.39
  (47 shorter events, 12.8 us)
Async XLA Ops:
  6.5 1.2 copy-start
  6.5 6.5 %copy-start.3 = (bf16[2048,512]{1,0:T(8,128)(2,1)S(1)}, bf16[2048,512]{1,0:T(8,128)(2,1)}, u32[]{:S(2)}) copy-start(bf16[2048,512]{1,0:T(8,128)(2,1)} %param.19) | copy-start | bytes 6291460
  6.5 82.3 %all-gather.2.cloned.1.call-start = ((), (), s32[]{:S(2)}) async-start(), calls=%async_computation | async-start | bytes 4718592 | tf_op jit(solution)/shard_map/all_gather | solution.py:490
  73.2 2.3 collective-permute-start
  75.6 13.2 %collective-permute-start.1 = (bf16[256,1024]{0,1:T(8,128)(2,1)S(1)}, bf16[256,1024]{0,1:T(8,128)(2,1)S(1)}, u32[]{:S(2)}, u32[]{:S(2)}) collective-permute-start(bf16[256,1024]{0,1:T(8,128)(2,1)S(1)} %bitcast.86), channel_id=1, source_target_pairs={{0,16},{16,0},{1,17},{17,1},{2,18},{18,2},{3,19},{19,3},{4,20},{20... | collective-permute-start | bytes 1572872 | tf_op jit(solution)/shard_map/ppermute | solution.py:512
  88.8 4.9 %copy-start.8 = (bf16[1024,2048]{1,0:T(8,128)(2,1)S(1)}, bf16[1024,2048]{1,0:T(8,128)(2,1)}, u32[]{:S(2)}) copy-start(bf16[1024,2048]{1,0:T(8,128)(2,1)} %all-gather.2.cloned.1.call-done) | copy-start | bytes 12582916
  92.5 2.8 %collective-permute-start.2 = (bf16[128,2048]{1,0:T(8,128)(2,1)S(1)}, bf16[128,2048]{1,0:T(8,128)(2,1)S(1)}, u32[]{:S(2)}, u32[]{:S(2)}) collective-permute-start(bf16[128,2048]{1,0:T(8,128)(2,1)S(1)} %slice.31), channel_id=1, source_target_pairs={{0,1},{1,0},{2,3},{3,2},{4,5},{5,4},{6,7},{7,6},{8,9},{9,8},{10,11... | collective-permute-start | bytes 1572872 | tf_op jit(solution)/shard_map/ppermute | solution.py:516
  93.8 2.9 %copy-start.6 = (s32[128,8]{0,1:T(8,128)S(1)}, s32[128,8]{0,1:T(8,128)}, u32[]{:S(2)}) copy-start(s32[128,8]{0,1:T(8,128)} %param.25) | copy-start | bytes 12292
  93.8 2.9 %copy-start.7 = (f32[128,8]{0,1:T(8,128)S(1)}, f32[128,8]{0,1:T(8,128)}, u32[]{:S(2)}) copy-start(f32[128,8]{0,1:T(8,128)} %param.26) | copy-start | bytes 12292
  93.8 14.8 %copy-start.4 = (bf16[128,2048]{1,0:T(8,128)(2,1)S(1)}, bf16[128,2048]{1,0:T(8,128)(2,1)}, u32[]{:S(2)}) copy-start(bf16[128,2048]{1,0:T(8,128)(2,1)} %param.22) | copy-start | bytes 1572868
  95.1 14.9 %copy-start.5 = (f32[2048]{0:T(1024)S(1)}, f32[2048]{0:T(1024)}, u32[]{:S(2)}) copy-start(f32[2048]{0:T(1024)} %param.24) | copy-start | bytes 24580
  95.1 2.1 collective-permute-start.4
  95.4 13.2 %collective-permute-start.3 = (bf16[128,2048]{1,0:T(8,128)(2,1)S(1)}, bf16[128,2048]{1,0:T(8,128)(2,1)S(1)}, u32[]{:S(2)}, u32[]{:S(2)}) collective-permute-start(bf16[128,2048]{1,0:T(8,128)(2,1)S(1)} %fusion.50), channel_id=1, source_target_pairs={{0,16},{16,0},{1,17},{17,1},{2,18},{18,2},{3,19},{19,3},{4,20},{20... | collective-permute-start | bytes 1572872 | tf_op jit(solution)/shard_map/ppermute | solution.py:522
  109.0 1.0 copy-start.2
  190.4 73.6 %copy-start.1 = (bf16[256,2048]{1,0:T(8,128)(2,1)S(1)}, bf16[256,2048]{1,0:T(8,128)(2,1)}, u32[]{:S(2)}) copy-start(bf16[256,2048]{1,0:T(8,128)(2,1)} %param.23) | copy-start | bytes 3145732
Sparse Core Ops, SparseCore 0:
  9.5 71.8 all-gather.1

commit v2 on v1

--- a/solution.py
+++ b/solution.py
@@ -181,7 +181,7 @@
 
 
 def sum_kernel(
-    count, parts, mixed, out, from_core, from_row, total, from_below, from_above,
+    count, parts, mixed, out, held, from_core, from_row, total, from_below, from_above,
     core_sem, row_sem, up_sem, down_sem,
 ):
     level, row, core, levels = place_of(count)
@@ -269,7 +269,7 @@
                 total[level_to, where, :] = base(slot, level_to, where).astype(jnp.bfloat16)
 
             def finish(where):
-                out[where, :] = mixed[where, :] + base(slot, level_to, where)
+                held[where, :] = mixed[where, :] + base(slot, level_to, where)
 
             tiles(finish)
             for neighbour, incoming, copy in (
@@ -281,9 +281,14 @@
                     copy(level_to).wait_recv()
 
                     def more(where):
-                        out[where, :] += incoming[level_to, where, :].astype(jnp.float32)
+                        held[where, :] += incoming[level_to, where, :].astype(jnp.float32)
 
                     tiles(more)
+
+            def rounded(where):
+                out[where, :] = held[where, :].astype(out.dtype)
+
+            tiles(rounded)
             return
         behind = level > 0 if way == 1 else level < levels - 1
         incoming, copy = (from_below, to_up) if way == 1 else (from_above, to_down)
@@ -333,10 +338,11 @@
 
     return pl.pallas_call(
         functools.partial(sum_kernel, count),
-        out_shape=jax.ShapeDtypeStruct(mixed.shape, jnp.float32),
+        out_shape=jax.ShapeDtypeStruct(mixed.shape, jnp.bfloat16),
         in_specs=[inside, inside],
         out_specs=inside,
         scratch_shapes=[
+            pltpu.VMEM(mixed.shape, jnp.float32),
             blocks(count // 2),
             blocks(levels),
             blocks(levels),
@@ -533,8 +539,7 @@
         down_weight,
         capacity,
     )
-    final = sum_rows(summed.reshape(devices, row_count, -1), mixed, devices)
-    return final.astype(jnp.bfloat16)
+    return sum_rows(summed.reshape(devices, row_count, -1), mixed, devices)
 
 
 def solution(mesh):

time: 276 us -> 276 us (level)
    unnamed x25 -> x26, local copies, waits for them, and re-layouts: 11.9 us -> 13.8 us
where the time goes in v2:
time: 276 us; the launch traced here: 271 us
  Pallas kernels  151 us (55%)
  matrix products  52.9 us (19%)
  waiting for transfers between devices  24.5 us (9%)
  local copies, waits for them, and re-layouts  16.1 us (6%)
  between operations  14.3 us (5%)
  other arithmetic  7.24 us (3%)
  starting transfers between devices  4.63 us (2%)
    pallas_call x1, Pallas kernels, sum_rows(): pl.pallas_call(functools.partial(sum_kernel, count), out_shape=jax.ShapeD...  71.4 us
    pallas_call x1, Pallas kernels, gather_rows(): pl.pallas_call(functools.partial(gather_kernel, count), out_shape=(jax.Sh...  52.4 us
    dot_general x4, matrix products, one_head(): jnp.einsum('rgk,kd->rgd', weights, value_head, preferred_element_type=jnp...  29.6 us
    pallas_call x1, Pallas kernels, run_experts(): pl.pallas_call(functools.partial(expert_kernel, capacity, slots, doubled...  27 us
    sub x4, matrix products, one_head(): weights = jnp.exp(scores - highest)  18.4 us
    unnamed x26, local copies, waits for them, and re-layouts  13.8 us
    ppermute x1, waiting for transfers between devices, body(): rows = lax.ppermute(rows, 'groups', ahead)  11.9 us
    ppermute x1, waiting for transfers between devices, body(): summed_rows = lax.ppermute(summed_rows.astype(jnp.bfloat16), 'groups', back)  11.3 us
  transfers between devices with their start and end apart: 6, of which 4 were waited for; matrix products, arithmetic and copies ran while one was open for 24% of the time, Pallas kernels for 0%

profile of v2, /device:TPU:13, one launch (start us, length us, event | category | flops | bytes accessed | tf_op | source)
XLA Modules:
  0.0 270.5 jit_solution(4384526711104813325)
XLA Ops:
  11.4 1.6 copy.15
  13.0 2.5 copy.16
  15.5 2.9 %copy.18 = bf16[2048,512]{0,1:T(8,128)(2,1)S(1)} copy(bf16[2048,512]{1,0:T(8,128)(2,1)} %param.20) | data formatting | bytes 4194304 | tf_op args[4]
  18.5 3.3 %pad_maximum_fusion = bf16[2176,512]{0,1:T(8,128)(2,1)} fusion(bf16[128,512]{0,1:T(8,128)(2,1)S(1)} %copy.17, bf16[2048,512]{0,1:T(8,128)(2,1)} %copy.16), kind=kLoop, calls=%fused_computation.32 | loop fusion | flops 4456448 | bytes 4456448 | tf_op jit(solution)/shard_map/concatenate | solution.py:484
  21.9 1.6 pad_maximum_fusion.1
  23.6 48.1 %while.10 = (s32[]{:T(128)}, bf16[4,128,8,128]{3,1,2,0:T(8,128)(2,1)}, pred[128,2176]{1,0:T(8,128)(4,1)S(1)}, bf16[4,128,8,128]{1,3,2,0:T(8,128)(2,1)S(1)}, bf16...) while((s32[]{:T(128)}, bf16[4,128,8,128]{3,1,2,0:T(8,128)(2,1)}, ...), condition=%wide.region_3.4_spmd, body=%wide.region_0.3_spmd.sunk | while | flops 1731466496 | bytes 3026005 | solution.py:31
  23.6 4.6 %fusion.77 = f32[128,8]{0,1:T(8,128)S(1)} fusion(pred[128,2176]{1,0:T(8,128)(4,1)S(1)} %get-tuple-element.119, bf16[4,2176,128]{1,2,0:T(8,128)(2,1)} %get-tuple-element.121, s32[]{:T(128)S(6)} %copy.33, bf16[4,128,8,128]{1,3,2,0:T(8,128)(2,1)S(1)} %get-tuple-element.120), kind=kOutput, calls=%fused_computation.57.clone.1 | convolution fusion | flops 579340416 | bytes 1102848 | tf_op jit(solution)/shard_map/while/body/eval_jaxpr/sub | solution.py:25
  28.2 7.4 %fusion.78 = bf16[4,128,8,128]{3,1,2,0:T(8,128)(2,1)} fusion(bf16[4,128,8,128]{3,1,2,0:T(8,128)(2,1)} %get-tuple-element.111, s32[]{:T(128)S(6)} %copy.33, f32[128,8]{0,1:T(8,128)S(1)} %fusion.77, bf16[4,2176,128]{1,2,0:T(8,128)(2,1)} %get-tuple-element.122, pred[128,2176]{1,0:T(8,128)(4,1)S(1)} %get-tuple-element.119, ...), kind=kOutput, calls=%fused_computation.12.clone.1 | convolution fusion | flops 1152126080 | bytes 1923072 | tf_op jit(solution)/shard_map/while/body/eval_jaxpr/rgk,kd->rgd/dot_general | solution.py:27
  35.6 4.6 %fusion.77 = f32[128,8]{0,1:T(8,128)S(1)} fusion(pred[128,2176]{1,0:T(8,128)(4,1)S(1)} %get-tuple-element.119, bf16[4,2176,128]{1,2,0:T(8,128)(2,1)} %get-tuple-element.121, s32[]{:T(128)S(6)} %copy.33, bf16[4,128,8,128]{1,3,2,0:T(8,128)(2,1)S(1)} %get-tuple-element.120), kind=kOutput, calls=%fused_computation.57.clone.1 | convolution fusion | flops 579340416 | bytes 1102848 | tf_op jit(solution)/shard_map/while/body/eval_jaxpr/sub | solution.py:25
  40.2 7.4 %fusion.78 = bf16[4,128,8,128]{3,1,2,0:T(8,128)(2,1)} fusion(bf16[4,128,8,128]{3,1,2,0:T(8,128)(2,1)} %get-tuple-element.111, s32[]{:T(128)S(6)} %copy.33, f32[128,8]{0,1:T(8,128)S(1)} %fusion.77, bf16[4,2176,128]{1,2,0:T(8,128)(2,1)} %get-tuple-element.122, pred[128,2176]{1,0:T(8,128)(4,1)S(1)} %get-tuple-element.119, ...), kind=kOutput, calls=%fused_computation.12.clone.1 | convolution fusion | flops 1152126080 | bytes 1923072 | tf_op jit(solution)/shard_map/while/body/eval_jaxpr/rgk,kd->rgd/dot_general | solution.py:27
  47.6 4.6 %fusion.77 = f32[128,8]{0,1:T(8,128)S(1)} fusion(pred[128,2176]{1,0:T(8,128)(4,1)S(1)} %get-tuple-element.119, bf16[4,2176,128]{1,2,0:T(8,128)(2,1)} %get-tuple-element.121, s32[]{:T(128)S(6)} %copy.33, bf16[4,128,8,128]{1,3,2,0:T(8,128)(2,1)S(1)} %get-tuple-element.120), kind=kOutput, calls=%fused_computation.57.clone.1 | convolution fusion | flops 579340416 | bytes 1102848 | tf_op jit(solution)/shard_map/while/body/eval_jaxpr/sub | solution.py:25
  52.2 7.4 %fusion.78 = bf16[4,128,8,128]{3,1,2,0:T(8,128)(2,1)} fusion(bf16[4,128,8,128]{3,1,2,0:T(8,128)(2,1)} %get-tuple-element.111, s32[]{:T(128)S(6)} %copy.33, f32[128,8]{0,1:T(8,128)S(1)} %fusion.77, bf16[4,2176,128]{1,2,0:T(8,128)(2,1)} %get-tuple-element.122, pred[128,2176]{1,0:T(8,128)(4,1)S(1)} %get-tuple-element.119, ...), kind=kOutput, calls=%fused_computation.12.clone.1 | convolution fusion | flops 1152126080 | bytes 1923072 | tf_op jit(solution)/shard_map/while/body/eval_jaxpr/rgk,kd->rgd/dot_general | solution.py:27
  59.6 4.6 %fusion.77 = f32[128,8]{0,1:T(8,128)S(1)} fusion(pred[128,2176]{1,0:T(8,128)(4,1)S(1)} %get-tuple-element.119, bf16[4,2176,128]{1,2,0:T(8,128)(2,1)} %get-tuple-element.121, s32[]{:T(128)S(6)} %copy.33, bf16[4,128,8,128]{1,3,2,0:T(8,128)(2,1)S(1)} %get-tuple-element.120), kind=kOutput, calls=%fused_computation.57.clone.1 | convolution fusion | flops 579340416 | bytes 1102848 | tf_op jit(solution)/shard_map/while/body/eval_jaxpr/sub | solution.py:25
  64.2 7.4 %fusion.78 = bf16[4,128,8,128]{3,1,2,0:T(8,128)(2,1)} fusion(bf16[4,128,8,128]{3,1,2,0:T(8,128)(2,1)} %get-tuple-element.111, s32[]{:T(128)S(6)} %copy.33, f32[128,8]{0,1:T(8,128)S(1)} %fusion.77, bf16[4,2176,128]{1,2,0:T(8,128)(2,1)} %get-tuple-element.122, pred[128,2176]{1,0:T(8,128)(4,1)S(1)} %get-tuple-element.119, ...), kind=kOutput, calls=%fused_computation.12.clone.1 | convolution fusion | flops 1152126080 | bytes 1923072 | tf_op jit(solution)/shard_map/while/body/eval_jaxpr/rgk,kd->rgd/dot_general | solution.py:27
  71.6 1.3 constant_dynamic-slice_fusion.1
  76.9 11.9 %collective-permute-done.1 = bf16[256,1024]{0,1:T(8,128)(2,1)S(1)} collective-permute-done((bf16[256,1024]{0,1:T(8,128)(2,1)S(1)}, bf16[256,1024]{0,1:T(8,128)(2,1)S(1)}, u32[]{:S(2)}, u32[]{:S(2)}) %collective-permute-start.1) | collective-permute-done | bytes 524320 | tf_op jit(solution)/shard_map/ppermute | solution.py:518
  88.8 3.6 %fusion.59 = f32[256,2048]{1,0:T(8,128)S(1)} fusion(bf16[256,1024]{0,1:T(8,128)(2,1)S(1)} %collective-permute-done.1, bf16[1024,2048]{1,0:T(8,128)(2,1)} %all-gather.2.cloned.1.call-done), kind=kOutput, calls=%fused_computation.58 | convolution fusion | flops 1073741824 | bytes 6815744 | tf_op jit(solution)/shard_map/dot_general | solution.py:519
  92.5 1.3 collective-permute-start.2
  93.8 1.3 fusion.60
  97.3 11.3 %collective-permute-done.3 = bf16[128,2048]{1,0:T(8,128)(2,1)S(1)} collective-permute-done((bf16[128,2048]{1,0:T(8,128)(2,1)S(1)}, bf16[128,2048]{1,0:T(8,128)(2,1)S(1)}, u32[]{:S(2)}, u32[]{:S(2)}) %collective-permute-start.3) | collective-permute-done | bytes 524320 | tf_op jit(solution)/shard_map/ppermute | solution.py:528
  110.9 52.4 %shard_map.136 = (bf16[16,128,2048]{2,1,0:T(8,128)(2,1)}, f32[16,16,128]{2,1,0:T(8,128)}) custom-call(bf16[128,2048]{1,0:T(8,128)(2,1)} %multiply_convert_fusion.rows_ref, f32[16,128]{1,0:T(8,128)} %pad_maximum_fusion.2.aux_ref), custom_call_target="tpu_custom_call" | custom-call | tf_op jit(solution)/shard_map/pallas_call | solution.py:166
  163.4 27.0 %shard_map.137 = bf16[2048,2048]{1,0:T(8,128)(2,1)} custom-call(f32[16,16,128]{2,1,0:T(8,128)} %get-tuple-element.40.aux, bf16[2048,2048]{1,0:T(8,128)(2,1)} %bitcast.78, bf16[4,2048,384]{2,1,0:T(8,128)(2,1)} %gate.1, bf16[4,2048,384]{2,1,0:T(8,128)(2,1)} %up.1, bf16[4,384,2048]{2,1,0:T(8,128)(2,1)} %down.1), custom_call_target="tpu_custom_call" | custom-call | tf_op jit(solution)/shard_map/pallas_call | solution.py:434
  190.4 71.4 %shard_map.138 = bf16[128,2048]{1,0:T(8,128)(2,1)} custom-call(bf16[16,128,2048]{2,1,0:T(8,128)(2,1)} %bitcast.77, f32[128,2048]{1,0:T(8,128)} %copy-done.2), custom_call_target="tpu_custom_call" | custom-call | tf_op jit(solution)/shard_map/pallas_call | solution.py:339
  261.8 1.9 copy.39
  (47 shorter events, 12.8 us)
Async XLA Ops:
  6.5 1.2 copy-start
  6.5 6.5 %copy-start.3 = (bf16[2048,512]{1,0:T(8,128)(2,1)S(1)}, bf16[2048,512]{1,0:T(8,128)(2,1)}, u32[]{:S(2)}) copy-start(bf16[2048,512]{1,0:T(8,128)(2,1)} %param.19) | copy-start | bytes 6291460
  6.5 82.3 %all-gather.2.cloned.1.call-start = ((), (), s32[]{:S(2)}) async-start(), calls=%async_computation | async-start | bytes 4718592 | tf_op jit(solution)/shard_map/all_gather | solution.py:496
  73.2 2.3 collective-permute-start
  75.6 13.2 %collective-permute-start.1 = (bf16[256,1024]{0,1:T(8,128)(2,1)S(1)}, bf16[256,1024]{0,1:T(8,128)(2,1)S(1)}, u32[]{:S(2)}, u32[]{:S(2)}) collective-permute-start(bf16[256,1024]{0,1:T(8,128)(2,1)S(1)} %bitcast.86), channel_id=1, source_target_pairs={{0,16},{16,0},{1,17},{17,1},{2,18},{18,2},{3,19},{19,3},{4,20},{20... | collective-permute-start | bytes 1572872 | tf_op jit(solution)/shard_map/ppermute | solution.py:518
  88.8 4.9 %copy-start.8 = (bf16[1024,2048]{1,0:T(8,128)(2,1)S(1)}, bf16[1024,2048]{1,0:T(8,128)(2,1)}, u32[]{:S(2)}) copy-start(bf16[1024,2048]{1,0:T(8,128)(2,1)} %all-gather.2.cloned.1.call-done) | copy-start | bytes 12582916
  92.5 2.8 %collective-permute-start.2 = (bf16[128,2048]{1,0:T(8,128)(2,1)S(1)}, bf16[128,2048]{1,0:T(8,128)(2,1)S(1)}, u32[]{:S(2)}, u32[]{:S(2)}) collective-permute-start(bf16[128,2048]{1,0:T(8,128)(2,1)S(1)} %slice.31), channel_id=1, source_target_pairs={{0,1},{1,0},{2,3},{3,2},{4,5},{5,4},{6,7},{7,6},{8,9},{9,8},{10,11... | collective-permute-start | bytes 1572872 | tf_op jit(solution)/shard_map/ppermute | solution.py:522
  93.8 2.9 %copy-start.6 = (s32[128,8]{0,1:T(8,128)S(1)}, s32[128,8]{0,1:T(8,128)}, u32[]{:S(2)}) copy-start(s32[128,8]{0,1:T(8,128)} %param.25) | copy-start | bytes 12292
  93.8 2.9 %copy-start.7 = (f32[128,8]{0,1:T(8,128)S(1)}, f32[128,8]{0,1:T(8,128)}, u32[]{:S(2)}) copy-start(f32[128,8]{0,1:T(8,128)} %param.26) | copy-start | bytes 12292
  93.8 14.8 %copy-start.4 = (bf16[128,2048]{1,0:T(8,128)(2,1)S(1)}, bf16[128,2048]{1,0:T(8,128)(2,1)}, u32[]{:S(2)}) copy-start(bf16[128,2048]{1,0:T(8,128)(2,1)} %param.22) | copy-start | bytes 1572868
  95.1 14.9 %copy-start.5 = (f32[2048]{0:T(1024)S(1)}, f32[2048]{0:T(1024)}, u32[]{:S(2)}) copy-start(f32[2048]{0:T(1024)} %param.24) | copy-start | bytes 24580
  95.1 2.1 collective-permute-start.4
  95.4 13.2 %collective-permute-start.3 = (bf16[128,2048]{1,0:T(8,128)(2,1)S(1)}, bf16[128,2048]{1,0:T(8,128)(2,1)S(1)}, u32[]{:S(2)}, u32[]{:S(2)}) collective-permute-start(bf16[128,2048]{1,0:T(8,128)(2,1)S(1)} %fusion.50), channel_id=1, source_target_pairs={{0,16},{16,0},{1,17},{17,1},{2,18},{18,2},{3,19},{19,3},{4,20},{20... | collective-permute-start | bytes 1572872 | tf_op jit(solution)/shard_map/ppermute | solution.py:528
  109.0 1.0 copy-start.2
  190.4 73.3 %copy-start.1 = (bf16[256,2048]{1,0:T(8,128)(2,1)S(1)}, bf16[256,2048]{1,0:T(8,128)(2,1)}, u32[]{:S(2)}) copy-start(bf16[256,2048]{1,0:T(8,128)(2,1)} %param.23) | copy-start | bytes 3145732
Sparse Core Ops, SparseCore 0:
  9.5 71.8 all-gather.1

commit v3 on v2

--- a/solution.py
+++ b/solution.py
@@ -235,8 +235,7 @@
 
         act(level, 0)
 
-    for row_to in (1 - row, row):
-        in_order(lambda level_to, way, row_to=row_to: to_core(level_to, row_to).start())
+    in_order(lambda level_to, way: to_core(level_to, 1 - row).start())
 
     def pass_row(level_to, way):
         slot = level_to * 2 + 1 - row
@@ -250,6 +249,7 @@
 
         tiles(add)
         to_row(level_to).start()
+        to_core(level_to, row).start()
 
     in_order(pass_row)
 

time: 276 us -> 276 us (level)
  no operation moved by 1% of the time
where the time goes in v3:
time: 276 us; the launch traced here: 271 us
  Pallas kernels  151 us (55%)
  matrix products  52.9 us (19%)
  waiting for transfers between devices  24.5 us (9%)
  local copies, waits for them, and re-layouts  16.1 us (6%)
  between operations  14.3 us (5%)
  other arithmetic  7.24 us (3%)
  starting transfers between devices  4.63 us (2%)
    pallas_call x1, Pallas kernels, sum_rows(): pl.pallas_call(functools.partial(sum_kernel, count), out_shape=jax.ShapeD...  71.4 us
    pallas_call x1, Pallas kernels, gather_rows(): pl.pallas_call(functools.partial(gather_kernel, count), out_shape=(jax.Sh...  52.4 us
    dot_general x4, matrix products, one_head(): jnp.einsum('rgk,kd->rgd', weights, value_head, preferred_element_type=jnp...  29.6 us
    pallas_call x1, Pallas kernels, run_experts(): pl.pallas_call(functools.partial(expert_kernel, capacity, slots, doubled...  27 us
    sub x4, matrix products, one_head(): weights = jnp.exp(scores - highest)  18.4 us
    unnamed x26, local copies, waits for them, and re-layouts  13.8 us
    ppermute x1, waiting for transfers between devices, body(): rows = lax.ppermute(rows, 'groups', ahead)  11.9 us
    ppermute x1, waiting for transfers between devices, body(): summed_rows = lax.ppermute(summed_rows.astype(jnp.bfloat16), 'groups', back)  11.3 us
  transfers between devices with their start and end apart: 6, of which 4 were waited for; matrix products, arithmetic and copies ran while one was open for 24% of the time, Pallas kernels for 0%

profile of v3, /device:TPU:13, one launch (start us, length us, event | category | flops | bytes accessed | tf_op | source)
XLA Modules:
  0.0 270.5 jit_solution(5652636653800223462)
XLA Ops:
  11.4 1.6 copy.15
  13.0 2.5 copy.16
  15.5 2.9 %copy.18 = bf16[2048,512]{0,1:T(8,128)(2,1)S(1)} copy(bf16[2048,512]{1,0:T(8,128)(2,1)} %param.20) | data formatting | bytes 4194304 | tf_op args[4]
  18.5 3.3 %pad_maximum_fusion = bf16[2176,512]{0,1:T(8,128)(2,1)} fusion(bf16[128,512]{0,1:T(8,128)(2,1)S(1)} %copy.17, bf16[2048,512]{0,1:T(8,128)(2,1)} %copy.16), kind=kLoop, calls=%fused_computation.32 | loop fusion | flops 4456448 | bytes 4456448 | tf_op jit(solution)/shard_map/concatenate | solution.py:484
  21.9 1.6 pad_maximum_fusion.1
  23.6 48.1 %while.10 = (s32[]{:T(128)}, bf16[4,128,8,128]{3,1,2,0:T(8,128)(2,1)}, pred[128,2176]{1,0:T(8,128)(4,1)S(1)}, bf16[4,128,8,128]{1,3,2,0:T(8,128)(2,1)S(1)}, bf16...) while((s32[]{:T(128)}, bf16[4,128,8,128]{3,1,2,0:T(8,128)(2,1)}, ...), condition=%wide.region_3.4_spmd, body=%wide.region_0.3_spmd.sunk | while | flops 1731466496 | bytes 3026005 | solution.py:31
  23.6 4.6 %fusion.77 = f32[128,8]{0,1:T(8,128)S(1)} fusion(pred[128,2176]{1,0:T(8,128)(4,1)S(1)} %get-tuple-element.119, bf16[4,2176,128]{1,2,0:T(8,128)(2,1)} %get-tuple-element.121, s32[]{:T(128)S(6)} %copy.33, bf16[4,128,8,128]{1,3,2,0:T(8,128)(2,1)S(1)} %get-tuple-element.120), kind=kOutput, calls=%fused_computation.57.clone.1 | convolution fusion | flops 579340416 | bytes 1102848 | tf_op jit(solution)/shard_map/while/body/eval_jaxpr/sub | solution.py:25
  28.2 7.4 %fusion.78 = bf16[4,128,8,128]{3,1,2,0:T(8,128)(2,1)} fusion(bf16[4,128,8,128]{3,1,2,0:T(8,128)(2,1)} %get-tuple-element.111, s32[]{:T(128)S(6)} %copy.33, f32[128,8]{0,1:T(8,128)S(1)} %fusion.77, bf16[4,2176,128]{1,2,0:T(8,128)(2,1)} %get-tuple-element.122, pred[128,2176]{1,0:T(8,128)(4,1)S(1)} %get-tuple-element.119, ...), kind=kOutput, calls=%fused_computation.12.clone.1 | convolution fusion | flops 1152126080 | bytes 1923072 | tf_op jit(solution)/shard_map/while/body/eval_jaxpr/rgk,kd->rgd/dot_general | solution.py:27
  35.6 4.6 %fusion.77 = f32[128,8]{0,1:T(8,128)S(1)} fusion(pred[128,2176]{1,0:T(8,128)(4,1)S(1)} %get-tuple-element.119, bf16[4,2176,128]{1,2,0:T(8,128)(2,1)} %get-tuple-element.121, s32[]{:T(128)S(6)} %copy.33, bf16[4,128,8,128]{1,3,2,0:T(8,128)(2,1)S(1)} %get-tuple-element.120), kind=kOutput, calls=%fused_computation.57.clone.1 | convolution fusion | flops 579340416 | bytes 1102848 | tf_op jit(solution)/shard_map/while/body/eval_jaxpr/sub | solution.py:25
  40.2 7.4 %fusion.78 = bf16[4,128,8,128]{3,1,2,0:T(8,128)(2,1)} fusion(bf16[4,128,8,128]{3,1,2,0:T(8,128)(2,1)} %get-tuple-element.111, s32[]{:T(128)S(6)} %copy.33, f32[128,8]{0,1:T(8,128)S(1)} %fusion.77, bf16[4,2176,128]{1,2,0:T(8,128)(2,1)} %get-tuple-element.122, pred[128,2176]{1,0:T(8,128)(4,1)S(1)} %get-tuple-element.119, ...), kind=kOutput, calls=%fused_computation.12.clone.1 | convolution fusion | flops 1152126080 | bytes 1923072 | tf_op jit(solution)/shard_map/while/body/eval_jaxpr/rgk,kd->rgd/dot_general | solution.py:27
  47.6 4.6 %fusion.77 = f32[128,8]{0,1:T(8,128)S(1)} fusion(pred[128,2176]{1,0:T(8,128)(4,1)S(1)} %get-tuple-element.119, bf16[4,2176,128]{1,2,0:T(8,128)(2,1)} %get-tuple-element.121, s32[]{:T(128)S(6)} %copy.33, bf16[4,128,8,128]{1,3,2,0:T(8,128)(2,1)S(1)} %get-tuple-element.120), kind=kOutput, calls=%fused_computation.57.clone.1 | convolution fusion | flops 579340416 | bytes 1102848 | tf_op jit(solution)/shard_map/while/body/eval_jaxpr/sub | solution.py:25
  52.2 7.4 %fusion.78 = bf16[4,128,8,128]{3,1,2,0:T(8,128)(2,1)} fusion(bf16[4,128,8,128]{3,1,2,0:T(8,128)(2,1)} %get-tuple-element.111, s32[]{:T(128)S(6)} %copy.33, f32[128,8]{0,1:T(8,128)S(1)} %fusion.77, bf16[4,2176,128]{1,2,0:T(8,128)(2,1)} %get-tuple-element.122, pred[128,2176]{1,0:T(8,128)(4,1)S(1)} %get-tuple-element.119, ...), kind=kOutput, calls=%fused_computation.12.clone.1 | convolution fusion | flops 1152126080 | bytes 1923072 | tf_op jit(solution)/shard_map/while/body/eval_jaxpr/rgk,kd->rgd/dot_general | solution.py:27
  59.6 4.6 %fusion.77 = f32[128,8]{0,1:T(8,128)S(1)} fusion(pred[128,2176]{1,0:T(8,128)(4,1)S(1)} %get-tuple-element.119, bf16[4,2176,128]{1,2,0:T(8,128)(2,1)} %get-tuple-element.121, s32[]{:T(128)S(6)} %copy.33, bf16[4,128,8,128]{1,3,2,0:T(8,128)(2,1)S(1)} %get-tuple-element.120), kind=kOutput, calls=%fused_computation.57.clone.1 | convolution fusion | flops 579340416 | bytes 1102848 | tf_op jit(solution)/shard_map/while/body/eval_jaxpr/sub | solution.py:25
  64.2 7.4 %fusion.78 = bf16[4,128,8,128]{3,1,2,0:T(8,128)(2,1)} fusion(bf16[4,128,8,128]{3,1,2,0:T(8,128)(2,1)} %get-tuple-element.111, s32[]{:T(128)S(6)} %copy.33, f32[128,8]{0,1:T(8,128)S(1)} %fusion.77, bf16[4,2176,128]{1,2,0:T(8,128)(2,1)} %get-tuple-element.122, pred[128,2176]{1,0:T(8,128)(4,1)S(1)} %get-tuple-element.119, ...), kind=kOutput, calls=%fused_computation.12.clone.1 | convolution fusion | flops 1152126080 | bytes 1923072 | tf_op jit(solution)/shard_map/while/body/eval_jaxpr/rgk,kd->rgd/dot_general | solution.py:27
  71.6 1.3 constant_dynamic-slice_fusion.1
  76.9 11.9 %collective-permute-done.1 = bf16[256,1024]{0,1:T(8,128)(2,1)S(1)} collective-permute-done((bf16[256,1024]{0,1:T(8,128)(2,1)S(1)}, bf16[256,1024]{0,1:T(8,128)(2,1)S(1)}, u32[]{:S(2)}, u32[]{:S(2)}) %collective-permute-start.1) | collective-permute-done | bytes 524320 | tf_op jit(solution)/shard_map/ppermute | solution.py:518
  88.8 3.6 %fusion.59 = f32[256,2048]{1,0:T(8,128)S(1)} fusion(bf16[256,1024]{0,1:T(8,128)(2,1)S(1)} %collective-permute-done.1, bf16[1024,2048]{1,0:T(8,128)(2,1)} %all-gather.2.cloned.1.call-done), kind=kOutput, calls=%fused_computation.58 | convolution fusion | flops 1073741824 | bytes 6815744 | tf_op jit(solution)/shard_map/dot_general | solution.py:519
  92.5 1.3 collective-permute-start.2
  93.8 1.3 fusion.60
  97.3 11.3 %collective-permute-done.3 = bf16[128,2048]{1,0:T(8,128)(2,1)S(1)} collective-permute-done((bf16[128,2048]{1,0:T(8,128)(2,1)S(1)}, bf16[128,2048]{1,0:T(8,128)(2,1)S(1)}, u32[]{:S(2)}, u32[]{:S(2)}) %collective-permute-start.3) | collective-permute-done | bytes 524320 | tf_op jit(solution)/shard_map/ppermute | solution.py:528
  110.9 52.4 %shard_map.136 = (bf16[16,128,2048]{2,1,0:T(8,128)(2,1)}, f32[16,16,128]{2,1,0:T(8,128)}) custom-call(bf16[128,2048]{1,0:T(8,128)(2,1)} %multiply_convert_fusion.rows_ref, f32[16,128]{1,0:T(8,128)} %pad_maximum_fusion.2.aux_ref), custom_call_target="tpu_custom_call" | custom-call | tf_op jit(solution)/shard_map/pallas_call | solution.py:166
  163.4 27.0 %shard_map.137 = bf16[2048,2048]{1,0:T(8,128)(2,1)} custom-call(f32[16,16,128]{2,1,0:T(8,128)} %get-tuple-element.40.aux, bf16[2048,2048]{1,0:T(8,128)(2,1)} %bitcast.78, bf16[4,2048,384]{2,1,0:T(8,128)(2,1)} %gate.1, bf16[4,2048,384]{2,1,0:T(8,128)(2,1)} %up.1, bf16[4,384,2048]{2,1,0:T(8,128)(2,1)} %down.1), custom_call_target="tpu_custom_call" | custom-call | tf_op jit(solution)/shard_map/pallas_call | solution.py:434
  190.4 71.4 %shard_map.138 = bf16[128,2048]{1,0:T(8,128)(2,1)} custom-call(bf16[16,128,2048]{2,1,0:T(8,128)(2,1)} %bitcast.77, f32[128,2048]{1,0:T(8,128)} %copy-done.2), custom_call_target="tpu_custom_call" | custom-call | tf_op jit(solution)/shard_map/pallas_call | solution.py:339
  261.8 1.9 copy.39
  (47 shorter events, 12.8 us)
Async XLA Ops:
  6.5 1.2 copy-start
  6.5 6.5 %copy-start.3 = (bf16[2048,512]{1,0:T(8,128)(2,1)S(1)}, bf16[2048,512]{1,0:T(8,128)(2,1)}, u32[]{:S(2)}) copy-start(bf16[2048,512]{1,0:T(8,128)(2,1)} %param.19) | copy-start | bytes 6291460
  6.5 82.3 %all-gather.2.cloned.1.call-start = ((), (), s32[]{:S(2)}) async-start(), calls=%async_computation | async-start | bytes 4718592 | tf_op jit(solution)/shard_map/all_gather | solution.py:496
  73.2 2.3 collective-permute-start
  75.6 13.2 %collective-permute-start.1 = (bf16[256,1024]{0,1:T(8,128)(2,1)S(1)}, bf16[256,1024]{0,1:T(8,128)(2,1)S(1)}, u32[]{:S(2)}, u32[]{:S(2)}) collective-permute-start(bf16[256,1024]{0,1:T(8,128)(2,1)S(1)} %bitcast.86), channel_id=1, source_target_pairs={{0,16},{16,0},{1,17},{17,1},{2,18},{18,2},{3,19},{19,3},{4,20},{20... | collective-permute-start | bytes 1572872 | tf_op jit(solution)/shard_map/ppermute | solution.py:518
  88.8 4.9 %copy-start.8 = (bf16[1024,2048]{1,0:T(8,128)(2,1)S(1)}, bf16[1024,2048]{1,0:T(8,128)(2,1)}, u32[]{:S(2)}) copy-start(bf16[1024,2048]{1,0:T(8,128)(2,1)} %all-gather.2.cloned.1.call-done) | copy-start | bytes 12582916
  92.5 2.8 %collective-permute-start.2 = (bf16[128,2048]{1,0:T(8,128)(2,1)S(1)}, bf16[128,2048]{1,0:T(8,128)(2,1)S(1)}, u32[]{:S(2)}, u32[]{:S(2)}) collective-permute-start(bf16[128,2048]{1,0:T(8,128)(2,1)S(1)} %slice.31), channel_id=1, source_target_pairs={{0,1},{1,0},{2,3},{3,2},{4,5},{5,4},{6,7},{7,6},{8,9},{9,8},{10,11... | collective-permute-start | bytes 1572872 | tf_op jit(solution)/shard_map/ppermute | solution.py:522
  93.8 2.9 %copy-start.6 = (s32[128,8]{0,1:T(8,128)S(1)}, s32[128,8]{0,1:T(8,128)}, u32[]{:S(2)}) copy-start(s32[128,8]{0,1:T(8,128)} %param.25) | copy-start | bytes 12292
  93.8 2.9 %copy-start.7 = (f32[128,8]{0,1:T(8,128)S(1)}, f32[128,8]{0,1:T(8,128)}, u32[]{:S(2)}) copy-start(f32[128,8]{0,1:T(8,128)} %param.26) | copy-start | bytes 12292
  93.8 14.8 %copy-start.4 = (bf16[128,2048]{1,0:T(8,128)(2,1)S(1)}, bf16[128,2048]{1,0:T(8,128)(2,1)}, u32[]{:S(2)}) copy-start(bf16[128,2048]{1,0:T(8,128)(2,1)} %param.22) | copy-start | bytes 1572868
  95.1 14.9 %copy-start.5 = (f32[2048]{0:T(1024)S(1)}, f32[2048]{0:T(1024)}, u32[]{:S(2)}) copy-start(f32[2048]{0:T(1024)} %param.24) | copy-start | bytes 24580
  95.1 2.1 collective-permute-start.4
  95.4 13.2 %collective-permute-start.3 = (bf16[128,2048]{1,0:T(8,128)(2,1)S(1)}, bf16[128,2048]{1,0:T(8,128)(2,1)S(1)}, u32[]{:S(2)}, u32[]{:S(2)}) collective-permute-start(bf16[128,2048]{1,0:T(8,128)(2,1)S(1)} %fusion.50), channel_id=1, source_target_pairs={{0,16},{16,0},{1,17},{17,1},{2,18},{18,2},{3,19},{19,3},{4,20},{20... | collective-permute-start | bytes 1572872 | tf_op jit(solution)/shard_map/ppermute | solution.py:528
  109.0 1.0 copy-start.2
  190.4 73.3 %copy-start.1 = (bf16[256,2048]{1,0:T(8,128)(2,1)S(1)}, bf16[256,2048]{1,0:T(8,128)(2,1)}, u32[]{:S(2)}) copy-start(bf16[256,2048]{1,0:T(8,128)(2,1)} %param.23) | copy-start | bytes 3145732
Sparse Core Ops, SparseCore 0:
  9.5 71.8 all-gather.1
